TPU v7x, 32 devices: a whole 2x2x4 slice. The times are simulated.
32 devices in a mesh: groups: 2 (over y), expert: 16 (over z, x, core), tensor: 1.
Axes of the slice: x: 2, y: 2, z: 4, core: 2. Of those that a mesh axis runs over, the one named last changes fastest.
Arguments:
- tokens: bfloat16 [512, 2048], P(('groups', 'expert')), parts along dimension 0, may hold values from -6 to 6
- expert_ids: int32 [512, 8], P(('groups', 'expert')), parts along dimension 0, may hold values from 0 to 15, all different within a row; in each aligned block of 16 rows (0 to 15, 16 to 31, ...) at most 16 rows name the same one
- keep_flags: int32 [512, 8], P(('groups', 'expert')), parts along dimension 0, may hold values 0 or 1
- router_weights: float32 [512, 8], P(('groups', 'expert')), parts along dimension 0, may hold values from 0.05 to 1
- grad_out: bfloat16 [512, 2048], P(('groups', 'expert'), 'tensor'), parts along dimension 0, may hold values from -6 to 6
- gate_weight: bfloat16 [16, 2048, 768], P('expert', None, 'tensor'), may hold values from -0.125 to 0.125
- up_weight: bfloat16 [16, 2048, 768], P('expert', None, 'tensor'), may hold values from -0.125 to 0.125
- down_weight: bfloat16 [16, 768, 2048], P('expert', 'tensor'), may hold values from -0.21875 to 0.21875
Outputs:
- combined: bfloat16 [512, 2048], P(('groups', 'expert'), 'tensor'), parts along dimension 0
- grad_tokens: bfloat16 [512, 2048], P(('groups', 'expert'), 'tensor'), parts along dimension 0
- grad_weights: float32 [512, 8], P(('groups', 'expert')), parts along dimension 0
There are 2 independent parts, one for each index of `groups`. A program takes and returns all parts, laid end to end along the dimension named above; an argument that names none is the same for every part. Nothing has to cross between parts.
Inputs may be any that keep to these rules, and one draw needn't show every extreme that they name: `expert_ids`: each row names 8 different experts and every expert is named by some row. Among the 16 rows of one device (aligned blocks) no expert is named more than 16 times, a bound that some block reaches.
All inputs are finite; a program needn't handle non-finite values. No bound on the sum of `keep_flags` on one device may be relied on, other than what follows from the above.
Results may differ from a plain program's by a relative error of at most 0.0071.
Values may be sent and summed in bfloat16 or wider, within the bound.
A program may use at most 64 MiB of HBM per device.

v0:
```python
import jax
import jax.numpy as jnp
from jax import lax
from jax.sharding import PartitionSpec as P


def route_tables(expert_ids, keep_flags, experts, capacity):
    tok_count, top_count = expert_ids.shape
    flat_ids = expert_ids.reshape(tok_count * top_count)
    onehot = (flat_ids[:, None] == jnp.arange(experts, dtype=jnp.int32)[None, :]).astype(jnp.int32)
    before = jnp.cumsum(onehot, axis=0) - onehot
    slot_rank = jnp.sum(before * onehot, axis=1)
    target = flat_ids * capacity + slot_rank
    picker = target[:, None] == jnp.arange(experts * capacity, dtype=jnp.int32)[None, :]
    kept = keep_flags.reshape(tok_count * top_count)[:, None] > 0
    sender = jnp.sum(
        (picker & kept).astype(jnp.bfloat16).reshape(tok_count, top_count, experts * capacity),
        axis=1,
    )
    return (picker.astype(jnp.bfloat16), sender)


def pack_rows(sender, source_cols, experts, capacity):
    packed = jnp.einsum("ts,td->sd", sender, source_cols, preferred_element_type=jnp.float32)
    return packed.astype(jnp.bfloat16).reshape(experts, capacity, source_cols.shape[1])


def local(
    tokens, expert_ids, keep_flags, router_weights, grad_out, gate_weight, up_weight, down_weight
):
    experts = lax.axis_size("expert")
    tok_count, top_count = expert_ids.shape
    capacity = min(tok_count, max(2, 2 * tok_count * top_count // experts))
    width = tokens.shape[1]
    width_half = grad_out.shape[1]
    gate_mat = gate_weight[0]
    up_mat = up_weight[0]
    down_mat = down_weight[0]
    picker, sender = route_tables(expert_ids, keep_flags, experts, capacity)
    keep_float = keep_flags.astype(jnp.float32)
    scale = keep_float * router_weights
    packed = pack_rows(sender, tokens, experts, capacity)
    received = lax.all_to_all(packed, "expert", split_axis=0, concat_axis=0, tiled=True)
    gate_pre = jnp.einsum("scd,dh->sch", received, gate_mat, preferred_element_type=jnp.float32)
    up_pre = jnp.einsum("scd,dh->sch", received, up_mat, preferred_element_type=jnp.float32)
    hidden = (jax.nn.silu(gate_pre) * up_pre).astype(jnp.bfloat16)
    partials = jnp.einsum("sch,hd->scd", hidden, down_mat, preferred_element_type=jnp.float32)
    partials, gate_pre, up_pre = (partials, gate_pre, up_pre)
    out_half = lax.psum_scatter(
        partials.astype(jnp.bfloat16), "tensor", scatter_dimension=2, tiled=True
    )
    returned = lax.all_to_all(out_half, "expert", split_axis=0, concat_axis=0, tiled=True).reshape(
        experts * capacity, width_half
    )
    out_assign = jnp.dot(picker, returned, preferred_element_type=jnp.float32).reshape(
        tok_count, top_count, width_half
    )
    combined = jnp.sum(scale[:, :, None] * out_assign, axis=1).astype(jnp.bfloat16)
    grad_float = grad_out.astype(jnp.float32)
    local_dots = keep_float * jnp.sum(grad_float[:, None, :] * out_assign, axis=2)
    grad_weights = lax.psum(local_dots, "tensor")
    grad_full = lax.all_gather(grad_out, "tensor", axis=1, tiled=True)
    grad_assign = (scale[:, :, None] * grad_full.astype(jnp.float32)[:, None, :]).astype(
        jnp.bfloat16
    )
    grad_assign = grad_assign.reshape(tok_count * top_count, width)
    grad_packed = jnp.einsum("as,ad->sd", picker, grad_assign, preferred_element_type=jnp.float32)
    grad_packed = grad_packed.astype(jnp.bfloat16).reshape(experts, capacity, width)
    grad_rows = lax.all_to_all(grad_packed, "expert", split_axis=0, concat_axis=0, tiled=True)
    grad_hidden = jnp.einsum("scd,hd->sch", grad_rows, down_mat, preferred_element_type=jnp.float32)
    sigmoid_gate = jax.nn.sigmoid(gate_pre)
    activated = gate_pre * sigmoid_gate
    grad_gate = (
        grad_hidden * up_pre * sigmoid_gate * (1.0 + gate_pre * (1.0 - sigmoid_gate))
    ).astype(jnp.bfloat16)
    grad_up = (grad_hidden * activated).astype(jnp.bfloat16)
    grad_part = jnp.einsum("sch,dh->scd", grad_gate, gate_mat, preferred_element_type=jnp.float32)
    grad_part = grad_part + jnp.einsum(
        "sch,dh->scd", grad_up, up_mat, preferred_element_type=jnp.float32
    )
    grad_half = lax.psum_scatter(
        grad_part.astype(jnp.bfloat16), "tensor", scatter_dimension=2, tiled=True
    )
    grad_back = lax.all_to_all(
        grad_half, "expert", split_axis=0, concat_axis=0, tiled=True
    ).reshape(experts * capacity, width_half)
    grad_picked = jnp.dot(picker, grad_back, preferred_element_type=jnp.float32).reshape(
        tok_count, top_count, width_half
    )
    grad_tokens = jnp.sum(grad_picked, axis=1).astype(jnp.bfloat16)
    return (combined, grad_tokens, grad_weights)


def solution(mesh):
    in_specs = (
        P(("groups", "expert"), None),
        P(("groups", "expert"), None),
        P(("groups", "expert"), None),
        P(("groups", "expert"), None),
        P(("groups", "expert"), "tensor"),
        P("expert", None, "tensor"),
        P("expert", None, "tensor"),
        P("expert", "tensor", None),
    )
    out_specs = (
        P(("groups", "expert"), "tensor"),
        P(("groups", "expert"), "tensor"),
        P(("groups", "expert"), None),
    )
    return jax.shard_map(local, mesh=mesh, in_specs=in_specs, out_specs=out_specs, check_vma=False)
```

profile of v0, /device:TPU:0, one launch (start us, length us, event | category | flops | bytes accessed | tf_op | source)
XLA Modules:
  0.0 128.0 jit_solution(9960942428415694899)
XLA Ops:
  0.7 0.8 broadcast_compare_fusion
  1.5 0.1 copy.31
  1.6 0.8 copy.29
  2.4 0.1 eq.62
  2.5 0.1 fusion.39
  2.6 0.2 reduce_window_sum.11
  2.8 0.2 select_reduce_fusion
  3.0 0.1 reduce_sum.51
  3.1 0.1 fusion.35
  3.2 2.3 %convolution_convert_fusion.1 = bf16[256,2048]{1,0:T(8,128)(2,1)} fusion(bf16[16,256]{1,0:T(8,128)(2,1)S(1)} %fusion.35, bf16[16,2048]{1,0:T(8,128)(2,1)} %param.8), kind=kOutput, calls=%fused_computation.16 | convolution fusion | flops 17301504 | bytes 1122304 | tf_op jit(solution)/shard_map/ts,td->sd/dot_general | solution.py:24
  5.5 7.4 %all-to-all-start = ((bf16[16,16,2048]{2,1,0:T(8,128)(2,1)}), bf16[16,16,2048]{2,1,0:T(8,128)(2,1)}, u32[]{:S(2)}, u32[]{:S(2)}) async-start(bf16[16,16,2048]{2,1,0:T(8,128)(2,1)} %bitcast.50), calls=%async_computation | async-start | bytes 2097152 | tf_op jit(solution)/shard_map/all_to_all | solution.py:43
  13.1 0.1 mul.89
  13.2 1.5 %convolution_convert_fusion = bf16[256,2048]{1,0:T(8,128)(2,1)} fusion(f32[16,2048]{1,0:T(8,128)S(1)} %convert_element_type.55, f32[128]{0:T(128)S(1)} %mul.89, s32[128]{0:T(128)S(1)} %multiply_add_fusion.1), kind=kOutput, calls=%fused_computation.14 | convolution fusion | flops 135299072 | bytes 1180672 | tf_op jit(solution)/shard_map/as,ad->sd/dot_general | solution.py:67
  14.8 21.2 %all-to-all-done = bf16[16,16,2048]{2,1,0:T(8,128)(2,1)} async-done(((bf16[16,16,2048]{2,1,0:T(8,128)(2,1)}), bf16[16,16,2048]{2,1,0:T(8,128)(2,1)}, u32[]{:S(2)}, u32[]{:S(2)}) %all-to-all-start) | async-done | bytes 1048608 | tf_op jit(solution)/shard_map/all_to_all | solution.py:43
  35.9 6.9 %all-to-all-start.2 = ((bf16[16,16,2048]{2,1,0:T(8,128)(2,1)}), bf16[16,16,2048]{2,1,0:T(8,128)(2,1)}, u32[]{:S(2)}, u32[]{:S(2)}) async-start(bf16[16,16,2048]{2,1,0:T(8,128)(2,1)} %bitcast.51), calls=%async_computation.2 | async-start | bytes 2097152 | tf_op jit(solution)/shard_map/all_to_all | solution.py:69
  42.9 3.3 %fusion.10 = f32[16,16,768]{2,1,0:T(8,128)S(1)} fusion(bf16[16,16,2048]{2,1,0:T(8,128)(2,1)} %all-to-all-done, bf16[1,2048,768]{2,1,0:T(8,128)(2,1)} %param.13), kind=kOutput, calls=%fused_computation.10 | convolution fusion | flops 805306368 | bytes 4980736 | tf_op jit(solution)/shard_map/scd,dh->sch/dot_general | solution.py:44
  46.2 2.5 %fusion.6 = f32[16,16,768]{2,1,0:T(8,128)S(1)} fusion(bf16[16,16,2048]{2,1,0:T(8,128)(2,1)} %all-to-all-done, bf16[1,2048,768]{2,1,0:T(8,128)(2,1)S(1)} %copy-done.4), kind=kOutput, calls=%fused_computation.6 | convolution fusion | flops 805306368 | bytes 4980736 | tf_op jit(solution)/shard_map/scd,dh->sch/dot_general | solution.py:45
  48.7 0.9 copy-done.9
  49.6 2.1 %fusion.18 = bf16[16,16,2048]{2,1,0:T(8,128)(2,1)} fusion(bf16[1,768,2048]{2,1,0:T(8,128)(2,1)S(1)} %copy-done, f32[16,16,768]{2,1,0:T(8,128)S(1)} %fusion.6, f32[16,16,768]{2,1,0:T(8,128)S(1)} %fusion.10), kind=kOutput, calls=%fused_computation.15 | convolution fusion | flops 807010304 | bytes 5767168 | tf_op jit(solution)/shard_map/sch,hd->scd/dot_general | solution.py:47
  51.7 14.2 %all-to-all-done.2 = bf16[16,16,2048]{2,1,0:T(8,128)(2,1)} async-done(((bf16[16,16,2048]{2,1,0:T(8,128)(2,1)}), bf16[16,16,2048]{2,1,0:T(8,128)(2,1)}, u32[]{:S(2)}, u32[]{:S(2)}) %all-to-all-start.2) | async-done | bytes 1048608 | tf_op jit(solution)/shard_map/all_to_all | solution.py:69
  65.9 6.9 %all-to-all-start.1 = ((bf16[16,16,2048]{2,1,0:T(8,128)(2,1)}), bf16[16,16,2048]{2,1,0:T(8,128)(2,1)}, u32[]{:S(2)}, u32[]{:S(2)}) async-start(bf16[16,16,2048]{2,1,0:T(8,128)(2,1)} %fusion.18), calls=%async_computation.1 | async-start | bytes 2097152 | tf_op jit(solution)/shard_map/all_to_all | solution.py:52
  72.8 2.4 %fusion = f32[16,16,768]{2,1,0:T(8,128)S(1)} fusion(bf16[16,16,2048]{2,1,0:T(8,128)(2,1)} %all-to-all-done.2, bf16[1,768,2048]{2,1,0:T(8,128)(2,1)S(1)} %copy-done), kind=kOutput, calls=%fused_computation | convolution fusion | flops 805306368 | bytes 4980736 | tf_op jit(solution)/shard_map/scd,hd->sch/dot_general | solution.py:70
  75.2 1.1 fusion.4
  76.3 0.8 copy-done.6
  77.1 0.2 copy-done.10
  77.3 2.1 %fusion.15 = bf16[16,16,2048]{2,1,0:T(8,128)(2,1)} fusion(f32[16,16,2048]{2,1,0:T(8,128)S(1)} %fusion.4, bf16[1,2048,768]{2,1,0:T(8,128)(2,1)S(1)} %copy-done.6, f32[16,16,768]{2,1,0:T(8,128)S(1)} %copy-done.8, f32[16,16,768]{2,1,0:T(8,128)S(1)} %fusion, f32[16,16,768]{2,1,0:T(8,128)S(1)} %copy-done.10), kind=kOutput, calls=%fused_computation.13 | convolution fusion | flops 808321024 | bytes 8650752 | tf_op jit(solution)/shard_map/sch,dh->scd/dot_general | solution.py:77
  79.4 16.4 %all-to-all-done.1 = bf16[16,16,2048]{2,1,0:T(8,128)(2,1)} async-done(((bf16[16,16,2048]{2,1,0:T(8,128)(2,1)}), bf16[16,16,2048]{2,1,0:T(8,128)(2,1)}, u32[]{:S(2)}, u32[]{:S(2)}) %all-to-all-start.1) | async-done | bytes 1048608 | tf_op jit(solution)/shard_map/all_to_all | solution.py:52
  95.8 6.9 %all-to-all-start.3 = ((bf16[16,16,2048]{2,1,0:T(8,128)(2,1)}), bf16[16,16,2048]{2,1,0:T(8,128)(2,1)}, u32[]{:S(2)}, u32[]{:S(2)}) async-start(bf16[16,16,2048]{2,1,0:T(8,128)(2,1)} %fusion.15), calls=%async_computation.3 | async-start | bytes 2097152 | tf_op jit(solution)/shard_map/all_to_all | solution.py:84
  102.7 2.5 %multiply_reduce_fusion = (f32[16,8]{1,0:T(8,128)S(1)}, bf16[16,2048]{1,0:T(8,128)(2,1)}) fusion(f32[16,2048]{1,0:T(8,128)S(1)} %convert_element_type.55, f32[16,8]{1,0:T(8,128)S(1)} %convert_multiply_fusion.1, bf16[256,2048,1]{1,0,2:T(8,128)(2,1)} %bitcast.9, s32[16,8]{1,0:T(8,128)S(1)} %multiply_add_fusion), kind=kOutput, calls=%fused_computation.20 | convolution fusion | flops 135266176 | bytes 1246720 | tf_op jit(solution)/shard_map/dot_general | solution.py:55
  105.2 0.7 copy.32
  105.9 19.8 %all-to-all-done.3 = bf16[16,16,2048]{2,1,0:T(8,128)(2,1)} async-done(((bf16[16,16,2048]{2,1,0:T(8,128)(2,1)}), bf16[16,16,2048]{2,1,0:T(8,128)(2,1)}, u32[]{:S(2)}, u32[]{:S(2)}) %all-to-all-start.3) | async-done | bytes 1048608 | tf_op jit(solution)/shard_map/all_to_all | solution.py:84
  125.7 2.3 %convolution_reduce_fusion = bf16[16,2048]{1,0:T(8,128)(2,1)} fusion(bf16[256,2048,1]{1,0,2:T(8,128)(2,1)} %bitcast.13, s32[16,8]{1,0:T(8,128)S(1)} %multiply_add_fusion), kind=kOutput, calls=%fused_computation.17 | convolution fusion | flops 134479872 | bytes 1114624 | tf_op jit(solution)/shard_map/dot_general | solution.py:87
  (26 shorter events, 0.2 us)
Async XLA Ops:
  0.6 49.0 %copy-start = (bf16[1,768,2048]{2,1,0:T(8,128)(2,1)S(1)}, bf16[1,768,2048]{2,1,0:T(8,128)(2,1)}, u32[]{:S(2)}) copy-start(bf16[1,768,2048]{2,1,0:T(8,128)(2,1)} %param.15) | copy-start | bytes 9437188
  0.6 12.3 %copy-start.2 = (s32[16,8]{0,1:T(8,128)S(1)}, s32[16,8]{0,1:T(8,128)}, u32[]{:S(2)}) copy-start(s32[16,8]{0,1:T(8,128)} %param.10) | copy-start | bytes 1540
  0.7 12.4 %copy-start.3 = (f32[16,8]{0,1:T(8,128)S(1)}, f32[16,8]{0,1:T(8,128)}, u32[]{:S(2)}) copy-start(f32[16,8]{0,1:T(8,128)} %param.11) | copy-start | bytes 1540
  0.7 12.5 %copy-start.1 = (bf16[16,2048]{1,0:T(8,128)(2,1)S(1)}, bf16[16,2048]{1,0:T(8,128)(2,1)}, u32[]{:S(2)}) copy-start(bf16[16,2048]{1,0:T(8,128)(2,1)} %param.12) | copy-start | bytes 196612
  5.5 30.4 %all-to-all-start = ((bf16[16,16,2048]{2,1,0:T(8,128)(2,1)}), bf16[16,16,2048]{2,1,0:T(8,128)(2,1)}, u32[]{:S(2)}, u32[]{:S(2)}) async-start(bf16[16,16,2048]{2,1,0:T(8,128)(2,1)} %bitcast.50), calls=%async_computation | async-start | bytes 2097152 | tf_op jit(solution)/shard_map/all_to_all | solution.py:43
  35.9 29.9 %all-to-all-start.2 = ((bf16[16,16,2048]{2,1,0:T(8,128)(2,1)}), bf16[16,16,2048]{2,1,0:T(8,128)(2,1)}, u32[]{:S(2)}, u32[]{:S(2)}) async-start(bf16[16,16,2048]{2,1,0:T(8,128)(2,1)} %bitcast.51), calls=%async_computation.2 | async-start | bytes 2097152 | tf_op jit(solution)/shard_map/all_to_all | solution.py:69
  42.9 3.4 %copy-start.4 = (bf16[1,2048,768]{2,1,0:T(8,128)(2,1)S(1)}, bf16[1,2048,768]{2,1,0:T(8,128)(2,1)}, u32[]{:S(2)}) copy-start(bf16[1,2048,768]{2,1,0:T(8,128)(2,1)} %param.14) | copy-start | bytes 9437188
  46.2 2.5 %copy-start.7 = (f32[16,16,768]{2,1,0:T(8,128)}, f32[16,16,768]{2,1,0:T(8,128)S(1)}, u32[]{:S(2)}) copy-start(f32[16,16,768]{2,1,0:T(8,128)S(1)} %fusion.10) | copy-start | bytes 2359300
  48.7 0.9 copy-start.9
  65.9 29.9 %all-to-all-start.1 = ((bf16[16,16,2048]{2,1,0:T(8,128)(2,1)}), bf16[16,16,2048]{2,1,0:T(8,128)(2,1)}, u32[]{:S(2)}, u32[]{:S(2)}) async-start(bf16[16,16,2048]{2,1,0:T(8,128)(2,1)} %fusion.18), calls=%async_computation.1 | async-start | bytes 2097152 | tf_op jit(solution)/shard_map/all_to_all | solution.py:52
  72.8 2.4 %copy-start.5 = (bf16[1,2048,768]{2,1,0:T(8,128)(2,1)S(1)}, bf16[1,2048,768]{2,1,0:T(8,128)(2,1)}, u32[]{:S(2)}) copy-start(bf16[1,2048,768]{2,1,0:T(8,128)(2,1)} %param.14) | copy-start | bytes 9437188
  72.8 2.4 %copy-start.8 = (f32[16,16,768]{2,1,0:T(8,128)S(1)}, f32[16,16,768]{2,1,0:T(8,128)}, u32[]{:S(2)}) copy-start(f32[16,16,768]{2,1,0:T(8,128)} %copy-done.7) | copy-start | bytes 2359300
  75.2 1.9 %copy-start.6 = (bf16[1,2048,768]{2,1,0:T(8,128)(2,1)S(1)}, bf16[1,2048,768]{2,1,0:T(8,128)(2,1)}, u32[]{:S(2)}) copy-start(bf16[1,2048,768]{2,1,0:T(8,128)(2,1)} %param.13) | copy-start | bytes 9437188
  75.2 2.1 %copy-start.10 = (f32[16,16,768]{2,1,0:T(8,128)S(1)}, f32[16,16,768]{2,1,0:T(8,128)}, u32[]{:S(2)}) copy-start(f32[16,16,768]{2,1,0:T(8,128)} %copy-done.9) | copy-start | bytes 2359300
  95.8 29.9 %all-to-all-start.3 = ((bf16[16,16,2048]{2,1,0:T(8,128)(2,1)}), bf16[16,16,2048]{2,1,0:T(8,128)(2,1)}, u32[]{:S(2)}, u32[]{:S(2)}) async-start(bf16[16,16,2048]{2,1,0:T(8,128)(2,1)} %fusion.15), calls=%async_computation.3 | async-start | bytes 2097152 | tf_op jit(solution)/shard_map/all_to_all | solution.py:84
where the time goes:
time: 130 us; the launch traced here: 128 us
  waiting for transfers between devices  71.5 us (55%)
  starting transfers between devices  28.2 us (22%)
  matrix products  22.1 us (17%)
  local copies, waits for them, and re-layouts  3.89 us (3%)
  other arithmetic  1.46 us (1%)
    all_to_all x1, waiting for transfers between devices, local(): lax.all_to_all(packed, 'expert', split_axis=0, concat_axis=0, tiled=True)  21.2 us
    all_to_all x1, waiting for transfers between devices, local(): lax.all_to_all(grad_half, 'expert', split_axis=0, concat_axis=0, tiled=True)  19.8 us
    all_to_all x1, waiting for transfers between devices, local(): lax.all_to_all(out_half, 'expert', split_axis=0, concat_axis=0, tiled=True)  16.4 us
    all_to_all x1, waiting for transfers between devices, local(): lax.all_to_all(grad_packed, 'expert', split_axis=0, concat_axis=0, tiled=...  14.2 us
    all_to_all x1, starting transfers between devices, local(): lax.all_to_all(packed, 'expert', split_axis=0, concat_axis=0, tiled=True)  7.41 us
    all_to_all x1, starting transfers between devices, local(): lax.all_to_all(grad_packed, 'expert', split_axis=0, concat_axis=0, tiled=...  6.92 us
    all_to_all x1, starting transfers between devices, local(): lax.all_to_all(out_half, 'expert', split_axis=0, concat_axis=0, tiled=True)  6.92 us
    all_to_all x1, starting transfers between devices, local(): lax.all_to_all(grad_half, 'expert', split_axis=0, concat_axis=0, tiled=True)  6.92 us
  transfers between devices with their start and end apart: 4, of which 4 were waited for; matrix products, arithmetic and copies ran while one was open for 14% of the time, Pallas kernels for 0%

commit v1 on v0

--- a/solution.py
+++ b/solution.py
@@ -1,7 +1,14 @@
+import functools
+
 import jax
 import jax.numpy as jnp
 from jax import lax
+from jax.experimental import pallas as pl
+from jax.experimental.pallas import tpu as pltpu
 from jax.sharding import PartitionSpec as P
+
+LANES = 128
+MESH_ID = pl.DeviceIdType.MESH
 
 
 def route_tables(expert_ids, keep_flags, experts, capacity):
@@ -25,7 +32,7 @@
     return packed.astype(jnp.bfloat16).reshape(experts, capacity, source_cols.shape[1])
 
 
-def local(
+def local_exchange(
     tokens, expert_ids, keep_flags, router_weights, grad_out, gate_weight, up_weight, down_weight
 ):
     experts = lax.axis_size("expert")
@@ -91,7 +98,296 @@
     return (combined, grad_tokens, grad_weights)
 
 
+def fused_kernel(depth, chunk, tokens, ids, keep, weights, cotangent, gate_hbm, up_hbm, down_hbm,
+                 combined, grad_tokens, grad_weights, rows, grads, gate_w, up_w, down_w, act, slope,
+                 hidden, d_gate, d_up, *rest):
+    count = len(chunk)
+    part, from_core, to_side, from_side, total, from_line = (
+        rest[i * count:(i + 1) * count] for i in range(6)
+    )
+    (w_sem, line_s, line_r, side_s, side_r, core_s, core_r,
+     a_s, a_r, b_s, b_r, c_s, c_r) = rest[6 * count:]
+    experts = lax.axis_size("expert")
+    me = lax.axis_index("expert")
+    core, side, line = lax.rem(me, 2), lax.rem(me // 2, 2), me // 4
+    tok_count, width = tokens.shape
+    hid = hidden.shape[1]
+    total_rows = 4 * depth * tok_count
+
+    def device(z, x, c):
+        return {"expert": (z * 2 + x) * 2 + c}
+
+    def behind(step):
+        return lax.rem(line + depth - step, depth)
+
+    def ahead(step):
+        return lax.rem(line + step, depth)
+
+    barrier = pltpu.get_barrier_semaphore()
+    peers = [device(ahead(step), side, core) for step in range(1, depth)]
+    side_peer = device(line, 1 - side, core)
+    core_peer = device(line, side, 1 - core)
+    for peer in peers + [side_peer, core_peer]:
+        pl.semaphore_signal(barrier, inc=1, device_id=peer, device_id_type=MESH_ID)
+
+    loads = [
+        pltpu.make_async_copy(source, target, w_sem.at[i])
+        for i, (source, target) in enumerate(
+            ((gate_hbm.at[0], gate_w), (up_hbm.at[0], up_w), (down_hbm.at[0], down_w))
+        )
+    ]
+    for load in loads:
+        load.start()
+
+    lane = lax.broadcasted_iota(jnp.int32, (tok_count, LANES), 1)
+    scale_own = jnp.zeros((tok_count, LANES), jnp.float32)
+    own_scale = keep[...].astype(jnp.float32) * weights[...]
+    for k in range(ids.shape[1]):
+        hit = lax.rem(lane, experts) == ids[:, k:k + 1]
+        scale_own = jnp.where(hit, own_scale[:, k:k + 1], scale_own)
+    high = scale_own.astype(jnp.bfloat16).astype(jnp.float32)
+    coded = jnp.where(lane < experts, high, scale_own - high)
+    coded = jnp.where(lane < 2 * experts, coded, 0.0)
+    rows[core, side, line, :, :width] = tokens[...]
+    rows[core, side, line, :, width:] = coded.astype(jnp.bfloat16)
+    grads[core, side, line] = cotangent[...]
+
+    pl.semaphore_wait(barrier, depth + 1)
+
+    sent = []
+
+    def send(source, target, s_sem, r_sem, peer):
+        copy = pltpu.make_async_remote_copy(
+            src_ref=source, dst_ref=target, send_sem=s_sem, recv_sem=r_sem,
+            device_id=peer, device_id_type=MESH_ID,
+        )
+        copy.start()
+        sent.append(copy)
+
+    def arrive(target, s_sem, r_sem, peer):
+        pltpu.make_async_remote_copy(
+            src_ref=target, dst_ref=target, send_sem=s_sem, recv_sem=r_sem,
+            device_id=peer, device_id_type=MESH_ID,
+        ).wait_recv()
+
+    def share_step(buf, which, step):
+        block = buf.at[core, side, behind(step)]
+        send(block, block, side_s.at[which, step], side_r.at[which, step], side_peer)
+        send(block, block, core_s.at[which, step], core_r.at[which, step], core_peer)
+
+    def gather_start(buf, which):
+        block = buf.at[core, side, line]
+        for step in range(1, depth):
+            send(block, block, line_s.at[which, step], line_r.at[which, step], peers[step - 1])
+        share_step(buf, which, 0)
+
+    def gather_line(buf, which):
+        for step in range(1, depth):
+            arrive(buf.at[core, side, behind(step)], line_s.at[which, step],
+                   line_r.at[which, step], peers[step - 1])
+            share_step(buf, which, step)
+
+    def gather_side(buf, which):
+        for step in range(depth):
+            block = buf.at[core, 1 - side, behind(step)]
+            arrive(block, side_s.at[which, step], side_r.at[which, step], side_peer)
+            send(block, block, core_s.at[which, depth + step], core_r.at[which, depth + step],
+                 core_peer)
+
+    def gather_end(buf, which):
+        for step in range(2 * depth):
+            x = side if step < depth else 1 - side
+            arrive(buf.at[1 - core, x, behind(step % depth)], core_s.at[which, step],
+                   core_r.at[which, step], core_peer)
+
+    gather_start(rows, 0)
+    gather_line(rows, 0)
+    gather_start(grads, 1)
+    gather_side(rows, 0)
+    gather_end(rows, 0)
+    loads[0].wait()
+    loads[1].wait()
+
+    tile = 256
+    data = rows[:, :, :, :, :width].reshape(total_rows, width)
+    lanes = lax.broadcasted_iota(jnp.int32, (total_rows, LANES), 1)
+    coded_all = rows[:, :, :, :, width:].reshape(total_rows, LANES).astype(jnp.float32)
+    mine = lax.rem(lanes, experts) == me
+    scale = jnp.sum(jnp.where(mine, coded_all, 0.0), axis=1, keepdims=True)
+
+    for t in range(hid // tile):
+        cols = slice(t * tile, (t + 1) * tile)
+        gate = jnp.dot(data, gate_w[:, cols], preferred_element_type=jnp.float32)
+        up = jnp.dot(data, up_w[:, cols], preferred_element_type=jnp.float32)
+        sig = jax.nn.sigmoid(gate)
+        activated = gate * sig
+        act[:, cols] = activated
+        slope[:, cols] = up * sig * (1.0 + gate * (1.0 - sig))
+        hidden[:, cols] = (activated * up).astype(jnp.bfloat16)
+        if t == 0:
+            gather_line(grads, 1)
+
+    def send_core(q):
+        send(part[q].at[1 - core], from_core[q], a_s.at[q], a_r.at[q], core_peer)
+
+    def send_side(q):
+        arrive(from_core[q], a_s.at[q], a_r.at[q], core_peer)
+        away = part[q][core, 1 - side].astype(jnp.float32)
+        away = away + from_core[q][1 - side].astype(jnp.float32)
+        to_side[q][...] = away.astype(jnp.bfloat16)
+        send(to_side[q], from_side[q], b_s.at[q], b_r.at[q], side_peer)
+
+    def send_line(q):
+        arrive(from_side[q], b_s.at[q], b_r.at[q], side_peer)
+        for step in range(1, depth):
+            z = ahead(step)
+            block = part[q][core, side, z].astype(jnp.float32)
+            block = block + from_core[q][side, z].astype(jnp.float32)
+            block = block + from_side[q][z].astype(jnp.float32)
+            total[q][step] = block.astype(jnp.bfloat16)
+            send(total[q].at[step], from_line[q].at[step], c_s.at[q, step], c_r.at[q, step],
+                 peers[step - 1])
+
+    def finish(q):
+        block = part[q][core, side, line].astype(jnp.float32)
+        block = block + from_core[q][side, line].astype(jnp.float32)
+        block = block + from_side[q][line].astype(jnp.float32)
+        for step in range(1, depth):
+            arrive(from_line[q].at[step], c_s.at[q, step], c_r.at[q, step], peers[step - 1])
+            block = block + from_line[q][step].astype(jnp.float32)
+        return block
+
+    half = count // 2
+    cuts = []
+    at = 0
+    for q in range(half):
+        cuts.append(slice(at, at + chunk[q]))
+        at += chunk[q]
+    shape = (2, 2, depth, tok_count)
+    loads[2].wait()
+    for q in range(half):
+        out = jnp.dot(hidden[...], down_w[:, cuts[q]], preferred_element_type=jnp.float32)
+        out = (scale * out).astype(jnp.bfloat16)
+        part[q][...] = out.reshape(shape + (chunk[q],))
+        send_core(q)
+        if q >= 1:
+            send_side(q - 1)
+    gather_side(grads, 1)
+    send_side(half - 1)
+    gather_end(grads, 1)
+
+    grad_data = grads[...].reshape(total_rows, width)
+    dots = jnp.zeros((total_rows, 1), jnp.float32)
+    contract = (((1,), (1,)), ((), ()))
+    for t in range(hid // tile):
+        cols = slice(t * tile, (t + 1) * tile)
+        back = lax.dot_general(grad_data, down_w[cols, :], contract,
+                               preferred_element_type=jnp.float32)
+        dots = dots + jnp.sum(back * hidden[:, cols].astype(jnp.float32), axis=1, keepdims=True)
+        back = back * scale
+        d_gate[:, cols] = (back * slope[:, cols]).astype(jnp.bfloat16)
+        d_up[:, cols] = (back * act[:, cols]).astype(jnp.bfloat16)
+    dots_high = dots.astype(jnp.bfloat16).astype(jnp.float32)
+    dots_coded = jnp.where(lanes < experts, dots_high, dots - dots_high)
+    dots_coded = jnp.where(mine & (lanes < 2 * experts), dots_coded, 0.0).astype(jnp.bfloat16)
+
+    for i in range(half):
+        q = half + i
+        wide = chunk[i]
+        grad = lax.dot_general(d_gate[...], gate_w[cuts[i], :], contract,
+                               preferred_element_type=jnp.float32)
+        grad = grad + lax.dot_general(d_up[...], up_w[cuts[i], :], contract,
+                                      preferred_element_type=jnp.float32)
+        part[q][:, :, :, :, :wide] = grad.astype(jnp.bfloat16).reshape(shape + (wide,))
+        if i == 0:
+            part[q][:, :, :, :, wide:] = dots_coded.reshape(shape + (LANES,))
+        send_core(q)
+        if i >= 1:
+            send_side(q - 1)
+        send_line(i)
+    send_side(count - 1)
+    for q in range(half, count):
+        send_line(q)
+    for q in range(half):
+        combined[:, cuts[q]] = finish(q).astype(jnp.bfloat16)
+    for i in range(half):
+        block = finish(half + i)
+        grad_tokens[:, cuts[i]] = block[:, :chunk[i]].astype(jnp.bfloat16)
+        if i == 0:
+            tail = block[:, chunk[i]:]
+            tail = jnp.where(lane < 2 * experts, tail, 0.0)
+            for k in range(ids.shape[1]):
+                hit = lax.rem(lane, experts) == ids[:, k:k + 1]
+                picked = jnp.sum(jnp.where(hit, tail, 0.0), axis=1, keepdims=True)
+                grad_weights[:, k:k + 1] = keep[:, k:k + 1].astype(jnp.float32) * picked
+    for copy in sent:
+        copy.wait_send()
+
+
+def local_fused(
+    tokens, expert_ids, keep_flags, router_weights, grad_out, gate_weight, up_weight, down_weight
+):
+    depth = lax.axis_size("expert") // 4
+    tok_count, width = tokens.shape
+    hid = gate_weight.shape[2]
+    total_rows = 4 * depth * tok_count
+    pieces = 4
+    each = width // pieces
+    chunk = [each] * (2 * pieces)
+    chunk[pieces] += LANES
+    bf16, f32 = jnp.bfloat16, jnp.float32
+
+    def blocks(*lead):
+        return [pltpu.VMEM(lead + (tok_count, wide), bf16) for wide in chunk]
+
+    scratch = [
+        pltpu.VMEM((2, 2, depth, tok_count, width + LANES), bf16),
+        pltpu.VMEM((2, 2, depth, tok_count, width), bf16),
+        pltpu.VMEM(gate_weight.shape[1:], bf16),
+        pltpu.VMEM(up_weight.shape[1:], bf16),
+        pltpu.VMEM(down_weight.shape[1:], bf16),
+        pltpu.VMEM((total_rows, hid), f32),
+        pltpu.VMEM((total_rows, hid), f32),
+        pltpu.VMEM((total_rows, hid), bf16),
+        pltpu.VMEM((total_rows, hid), bf16),
+        pltpu.VMEM((total_rows, hid), bf16),
+        *blocks(2, 2, depth),
+        *blocks(2, depth),
+        *blocks(depth),
+        *blocks(depth),
+        *blocks(depth),
+        *blocks(depth),
+    ]
+    sems = [(3,)] + [(2, depth)] * 4 + [(2, 2 * depth)] * 2
+    sems += [(len(chunk),)] * 4 + [(len(chunk), depth)] * 2
+    scratch += [pltpu.SemaphoreType.DMA(dims) for dims in sems]
+    vmem = pl.BlockSpec(memory_space=pltpu.VMEM)
+    far = pl.BlockSpec(memory_space=pl.ANY)
+    return pl.pallas_call(
+        functools.partial(fused_kernel, depth, chunk),
+        out_shape=(
+            jax.ShapeDtypeStruct(tokens.shape, bf16),
+            jax.ShapeDtypeStruct(tokens.shape, bf16),
+            jax.ShapeDtypeStruct(router_weights.shape, f32),
+        ),
+        in_specs=[vmem] * 5 + [far] * 3,
+        out_specs=(vmem, vmem, vmem),
+        scratch_shapes=scratch,
+        compiler_params=pltpu.CompilerParams(
+            collective_id=0, has_side_effects=True, vmem_limit_bytes=56 * 1024 * 1024
+        ),
+        cost_estimate=pl.CostEstimate(
+            flops=12 * total_rows * width * hid,
+            bytes_accessed=6 * width * hid,
+            transcendentals=total_rows * hid,
+        ),
+    )(tokens, expert_ids, keep_flags, router_weights, grad_out, gate_weight, up_weight, down_weight)
+
+
 def solution(mesh):
+    sizes = mesh.shape
+    dense = sizes["tensor"] == 1 and sizes["expert"] % 4 == 0 and 8 <= sizes["expert"] <= 32
+    local = local_fused if dense else local_exchange
     in_specs = (
         P(("groups", "expert"), None),
         P(("groups", "expert"), None),

time: 130 us -> 53.8 us (0.41); the launches traced: 128 us -> 53.4 us
  waiting for transfers between devices: 71.5 us -> 0 us
  Pallas kernels: 0 us -> 44.4 us
  starting transfers between devices: 28.2 us -> 0 us
  matrix products: 22.1 us -> 0 us
  local copies, waits for them, and re-layouts: 3.89 us -> 8.36 us
  other arithmetic: 1.46 us -> 0 us
    all_to_all x4 -> x0, waiting for transfers between devices: 71.5 us -> none  [the longest x1 21.2 us: local(): lax.all_to_all(packed, 'expert', split_axis=0, concat_axis=0, tiled=True)]
    pallas_call x0 -> x1, Pallas kernels: none -> 44.4 us  [local_fused(): pl.pallas_call(functools.partial(fused_kernel, depth, chunk), out_shape=(...]
    all_to_all x4 -> x0, starting transfers between devices: 28.2 us -> none  [the longest x1 7.41 us: local(): lax.all_to_all(packed, 'expert', split_axis=0, concat_axis=0, tiled=True)]
    dot_general x10 -> x0, matrix products: 22.1 us -> none  [the longest x1 3.33 us: local(): jnp.einsum('scd,dh->sch', received, gate_mat, preferred_element_type=jnp....]
    unnamed x26 -> x5, local copies, waits for them, and re-layouts: 3.55 us -> 7.01 us
    pallas_call x0 -> x1, local copies, waits for them, and re-layouts: none -> 1.36 us  [local_fused(): pl.pallas_call(functools.partial(fused_kernel, depth, chunk), out_shape=(...]
  transfers between devices with their start and end apart: 4 -> 0, of which waited for: 4 -> 0; matrix products, arithmetic and copies ran while one was open for 14% -> 0% of each run, Pallas kernels for 0% -> 0%
where the time goes in v1:
time: 53.8 us; the launch traced here: 53.4 us
  Pallas kernels  44.4 us (83%)
  local copies, waits for them, and re-layouts  8.36 us (16%)
  between operations  0.64 us (1%)
    pallas_call x1, Pallas kernels, local_fused(): pl.pallas_call(functools.partial(fused_kernel, depth, chunk), out_shape=(...  44.4 us
    unnamed x5, local copies, waits for them, and re-layouts  7.01 us
    pallas_call x1, local copies, waits for them, and re-layouts, local_fused(): pl.pallas_call(functools.partial(fused_kernel, depth, chunk), out_shape=(...  1.36 us

profile of v1, /device:TPU:0, one launch (start us, length us, event | category | flops | bytes accessed | tf_op | source)
XLA Modules:
  0.0 53.4 jit_solution(8180979739989194527)
XLA Ops:
  0.6 1.4 %copy.11.ids = s32[16,8]{1,0:T(8,128)} copy(s32[16,8]{0,1:T(8,128)} %param.9) | data formatting | bytes 1024 | tf_op args[1]
  2.0 1.4 %copy.12.keep = s32[16,8]{1,0:T(8,128)} copy(s32[16,8]{0,1:T(8,128)} %param.10) | data formatting | bytes 1024 | tf_op args[2]
  3.3 1.4 %copy.13.weights = f32[16,8]{1,0:T(8,128)} copy(f32[16,8]{0,1:T(8,128)} %param.11) | data formatting | bytes 1024 | tf_op args[3]
  4.7 44.4 %shard_map.103 = (bf16[16,2048]{1,0:T(8,128)(2,1)}, bf16[16,2048]{1,0:T(8,128)(2,1)}, f32[16,8]{1,0:T(8,128)}) custom-call(bf16[16,2048]{1,0:T(8,128)(2,1)} %tokens.1, s32[16,8]{1,0:T(8,128)} %copy.11.ids, s32[16,8]{1,0:T(8,128)} %copy.12.keep, f32[16,8]{1,0:T(8,128)} %copy.13.weights, bf16[16,2048]{1,0:T(8,128)(2,1)} %cotangent.1, ...), custom_call_target="tpu_custom_call" | custom-call | flops 4831838208 | bytes 9437184 | tf_op jit(solution)/shard_map/pallas_call | solution.py:366
  49.1 1.4 %copy.14 = f32[16,8]{0,1:T(8,128)} copy(f32[16,8]{1,0:T(8,128)} %get-tuple-element.5) | data formatting | bytes 1024 | tf_op jit(solution)/shard_map/pallas_call | solution.py:366
  50.5 1.5 %copy.17 = bf16[16,2048]{1,0:T(8,128)(2,1)} copy(bf16[16,2048]{1,0:T(8,128)(2,1)} %get-tuple-element.9) | data formatting | bytes 131072
  52.0 1.5 %copy.18 = bf16[16,2048]{1,0:T(8,128)(2,1)} copy(bf16[16,2048]{1,0:T(8,128)(2,1)} %get-tuple-element.10) | data formatting | bytes 131072

commit v2 on v1

--- a/solution.py
+++ b/solution.py
@@ -140,11 +140,12 @@
         load.start()
 
     lane = lax.broadcasted_iota(jnp.int32, (tok_count, LANES), 1)
-    scale_own = jnp.zeros((tok_count, LANES), jnp.float32)
+    place = lax.rem(lax.broadcasted_iota(jnp.int32, (LANES, tok_count), 0), experts)
     own_scale = keep[...].astype(jnp.float32) * weights[...]
-    for k in range(ids.shape[1]):
-        hit = lax.rem(lane, experts) == ids[:, k:k + 1]
-        scale_own = jnp.where(hit, own_scale[:, k:k + 1], scale_own)
+    scale_own = jnp.zeros((LANES, tok_count), jnp.float32)
+    for k in range(ids.shape[0]):
+        scale_own = jnp.where(place == ids[k:k + 1, :], own_scale[k:k + 1, :], scale_own)
+    scale_own = scale_own.T
     high = scale_own.astype(jnp.bfloat16).astype(jnp.float32)
     coded = jnp.where(lane < experts, high, scale_own - high)
     coded = jnp.where(lane < 2 * experts, coded, 0.0)
@@ -315,13 +316,22 @@
         grad_tokens[:, cuts[i]] = block[:, :chunk[i]].astype(jnp.bfloat16)
         if i == 0:
             tail = block[:, chunk[i]:]
-            tail = jnp.where(lane < 2 * experts, tail, 0.0)
-            for k in range(ids.shape[1]):
-                hit = lax.rem(lane, experts) == ids[:, k:k + 1]
-                picked = jnp.sum(jnp.where(hit, tail, 0.0), axis=1, keepdims=True)
-                grad_weights[:, k:k + 1] = keep[:, k:k + 1].astype(jnp.float32) * picked
+            tail = jnp.where(lane < 2 * experts, tail, 0.0).T
+            for k in range(ids.shape[0]):
+                picked = jnp.where(place == ids[k:k + 1, :], tail, 0.0)
+                picked = jnp.sum(picked, axis=0, keepdims=True)
+                grad_weights[k:k + 1, :] = keep[k:k + 1, :].astype(jnp.float32) * picked
     for copy in sent:
         copy.wait_send()
+
+
+def store_kernel(*refs):
+    sem = refs[-1]
+    copies = [pltpu.make_async_copy(refs[i], refs[3 + i], sem.at[i]) for i in range(3)]
+    for copy in copies:
+        copy.start()
+    for copy in copies:
+        copy.wait()
 
 
 def local_fused(
@@ -363,12 +373,12 @@
     scratch += [pltpu.SemaphoreType.DMA(dims) for dims in sems]
     vmem = pl.BlockSpec(memory_space=pltpu.VMEM)
     far = pl.BlockSpec(memory_space=pl.ANY)
-    return pl.pallas_call(
+    results = pl.pallas_call(
         functools.partial(fused_kernel, depth, chunk),
         out_shape=(
             jax.ShapeDtypeStruct(tokens.shape, bf16),
             jax.ShapeDtypeStruct(tokens.shape, bf16),
-            jax.ShapeDtypeStruct(router_weights.shape, f32),
+            jax.ShapeDtypeStruct(router_weights.shape[::-1], f32),
         ),
         in_specs=[vmem] * 5 + [far] * 3,
         out_specs=(vmem, vmem, vmem),
@@ -381,7 +391,16 @@
             bytes_accessed=6 * width * hid,
             transcendentals=total_rows * hid,
         ),
-    )(tokens, expert_ids, keep_flags, router_weights, grad_out, gate_weight, up_weight, down_weight)
+    )(tokens, expert_ids.T, keep_flags.T, router_weights.T, grad_out, gate_weight, up_weight,
+      down_weight)
+    combined, grad_tokens, grad_weights = pl.pallas_call(
+        store_kernel,
+        out_shape=tuple(jax.ShapeDtypeStruct(r.shape, r.dtype) for r in results),
+        in_specs=[far] * 3,
+        out_specs=(far,) * 3,
+        scratch_shapes=[pltpu.SemaphoreType.DMA((3,))],
+    )(*results)
+    return combined, grad_tokens, grad_weights.T
 
 
 def solution(mesh):

time: 53.8 us -> 50.4 us (0.937)
  local copies, waits for them, and re-layouts: 8.36 us -> 0 us
  Pallas kernels: 44.4 us -> 49.6 us
    unnamed x5 -> x0, local copies, waits for them, and re-layouts: 7.01 us -> none
    pallas_call x0 -> x1, Pallas kernels: none -> 5.22 us  [local_fused(): pl.pallas_call(store_kernel, out_shape=tuple((jax.ShapeDtypeStruct(r.shap...]
    pallas_call x1 -> x0, local copies, waits for them, and re-layouts: 1.36 us -> none  [local_fused(): pl.pallas_call(functools.partial(fused_kernel, depth, chunk), out_shape=(...]
where the time goes in v2:
time: 50.4 us; the launch traced here: 50.3 us
  Pallas kernels  49.6 us (98%)
  between operations  0.64 us (1%)
    pallas_call x1, Pallas kernels, local_fused(): pl.pallas_call(functools.partial(fused_kernel, depth, chunk), out_shape=(...  44.4 us
    pallas_call x1, Pallas kernels, local_fused(): pl.pallas_call(store_kernel, out_shape=tuple((jax.ShapeDtypeStruct(r.shap...  5.22 us

profile of v2, /device:TPU:0, one launch (start us, length us, event | category | flops | bytes accessed | tf_op | source)
XLA Modules:
  0.0 50.3 jit_solution(7509102474694680035)
XLA Ops:
  0.6 44.4 %shard_map.103 = (bf16[16,2048]{1,0:T(8,128)(2,1)}, bf16[16,2048]{1,0:T(8,128)(2,1)}, f32[8,16]{1,0:T(8,128)}) custom-call(bf16[16,2048]{1,0:T(8,128)(2,1)} %tokens.1, s32[8,16]{1,0:T(8,128)} %bitcast.4, s32[8,16]{1,0:T(8,128)} %bitcast.5, f32[8,16]{1,0:T(8,128)} %bitcast.6, bf16[16,2048]{1,0:T(8,128)(2,1)} %cotangent.1, bf16[1,2048,768]{2,1,0:T(8,128)(2,1)} %gate_hbm.1, ...), custom_call_target="tpu_custom_call" | custom-call | flops 4831838208 | bytes 9437184 | tf_op jit(solution)/shard_map/pallas_call | solution.py:376
  45.1 5.2 %shard_map.104 = (bf16[16,2048]{1,0:T(8,128)(2,1)}, bf16[16,2048]{1,0:T(8,128)(2,1)}, f32[8,16]{1,0:T(8,128)}) custom-call(bf16[16,2048]{1,0:T(8,128)(2,1)} %get-tuple-element.9.refs_0_, bf16[16,2048]{1,0:T(8,128)(2,1)} %get-tuple-element.10.refs_1_, f32[8,16]{1,0:T(8,128)} %get-tuple-element.11.refs_2_), custom_call_target="tpu_custom_call" | custom-call | tf_op jit(solution)/shard_map/pallas_call | solution.py:396

commit v3 on v2

--- a/solution.py
+++ b/solution.py
@@ -118,10 +118,10 @@
         return {"expert": (z * 2 + x) * 2 + c}
 
     def behind(step):
-        return lax.rem(line + depth - step, depth)
-
-    def ahead(step):
-        return lax.rem(line + step, depth)
+        pairs = (line, line + 1 - 2 * lax.rem(line, 2), lax.rem(line + 2, 4), 3 - line)
+        return pairs[step]
+
+    ahead = behind
 
     barrier = pltpu.get_barrier_semaphore()
     peers = [device(ahead(step), side, core) for step in range(1, depth)]
@@ -178,9 +178,9 @@
 
     def gather_start(buf, which):
         block = buf.at[core, side, line]
+        share_step(buf, which, 0)
         for step in range(1, depth):
             send(block, block, line_s.at[which, step], line_r.at[which, step], peers[step - 1])
-        share_step(buf, which, 0)
 
     def gather_line(buf, which):
         for step in range(1, depth):
@@ -205,6 +205,7 @@
     gather_line(rows, 0)
     gather_start(grads, 1)
     gather_side(rows, 0)
+    gather_line(grads, 1)
     gather_end(rows, 0)
     loads[0].wait()
     loads[1].wait()
@@ -225,8 +226,6 @@
         act[:, cols] = activated
         slope[:, cols] = up * sig * (1.0 + gate * (1.0 - sig))
         hidden[:, cols] = (activated * up).astype(jnp.bfloat16)
-        if t == 0:
-            gather_line(grads, 1)
 
     def send_core(q):
         send(part[q].at[1 - core], from_core[q], a_s.at[q], a_r.at[q], core_peer)
@@ -326,12 +325,8 @@
 
 
 def store_kernel(*refs):
-    sem = refs[-1]
-    copies = [pltpu.make_async_copy(refs[i], refs[3 + i], sem.at[i]) for i in range(3)]
-    for copy in copies:
-        copy.start()
-    for copy in copies:
-        copy.wait()
+    for i in range(3):
+        refs[3 + i][...] = refs[i][...]
 
 
 def local_fused(
@@ -396,16 +391,15 @@
     combined, grad_tokens, grad_weights = pl.pallas_call(
         store_kernel,
         out_shape=tuple(jax.ShapeDtypeStruct(r.shape, r.dtype) for r in results),
-        in_specs=[far] * 3,
-        out_specs=(far,) * 3,
-        scratch_shapes=[pltpu.SemaphoreType.DMA((3,))],
+        in_specs=[vmem] * 3,
+        out_specs=(vmem,) * 3,
     )(*results)
     return combined, grad_tokens, grad_weights.T
 
 
 def solution(mesh):
     sizes = mesh.shape
-    dense = sizes["tensor"] == 1 and sizes["expert"] % 4 == 0 and 8 <= sizes["expert"] <= 32
+    dense = sizes["tensor"] == 1 and sizes["expert"] == 16
     local = local_fused if dense else local_exchange
     in_specs = (
         P(("groups", "expert"), None),

time: 50.4 us -> 45.8 us (0.909)
  Pallas kernels: 49.6 us -> 45 us
    pallas_call x1, Pallas kernels: 5.22 us -> 1.53 us  [local_fused(): pl.pallas_call(store_kernel, out_shape=tuple((jax.ShapeDtypeStruct(r.shap...]
    pallas_call x1, Pallas kernels: 44.4 us -> 43.4 us  [local_fused(): pl.pallas_call(functools.partial(fused_kernel, depth, chunk), out_shape=(...]
where the time goes in v3:
time: 45.8 us; the launch traced here: 45.6 us
  Pallas kernels  45 us (98%)
  between operations  0.64 us (1%)
    pallas_call x1, Pallas kernels, local_fused(): pl.pallas_call(functools.partial(fused_kernel, depth, chunk), out_shape=(...  43.4 us
    pallas_call x1, Pallas kernels, local_fused(): pl.pallas_call(store_kernel, out_shape=tuple((jax.ShapeDtypeStruct(r.shap...  1.53 us

profile of v3, /device:TPU:0, one launch (start us, length us, event | category | flops | bytes accessed | tf_op | source)
XLA Modules:
  0.0 45.6 jit_solution(6175683374837364419)
XLA Ops:
  0.6 43.4 %shard_map.103 = (bf16[16,2048]{1,0:T(8,128)(2,1)}, bf16[16,2048]{1,0:T(8,128)(2,1)}, f32[8,16]{1,0:T(8,128)}) custom-call(bf16[16,2048]{1,0:T(8,128)(2,1)} %tokens.1, s32[8,16]{1,0:T(8,128)} %bitcast.4, s32[8,16]{1,0:T(8,128)} %bitcast.5, f32[8,16]{1,0:T(8,128)} %bitcast.6, bf16[16,2048]{1,0:T(8,128)(2,1)} %cotangent.1, bf16[1,2048,768]{2,1,0:T(8,128)(2,1)} %gate_hbm.1, ...), custom_call_target="tpu_custom_call" | custom-call | flops 4831838208 | bytes 9437184 | tf_op jit(solution)/shard_map/pallas_call | solution.py:371
  44.1 1.5 %shard_map.104 = (bf16[16,2048]{1,0:T(8,128)(2,1)}, bf16[16,2048]{1,0:T(8,128)(2,1)}, f32[8,16]{1,0:T(8,128)}) custom-call(bf16[16,2048]{1,0:T(8,128)(2,1)} %get-tuple-element.9.refs_0_, bf16[16,2048]{1,0:T(8,128)(2,1)} %get-tuple-element.10.refs_1_, f32[8,16]{1,0:T(8,128)} %get-tuple-element.11.refs_2_), custom_call_target="tpu_custom_call" | custom-call | tf_op jit(solution)/shard_map/pallas_call | solution.py:391

commit v4 on v3

--- a/solution.py
+++ b/solution.py
@@ -270,10 +270,9 @@
         out = (scale * out).astype(jnp.bfloat16)
         part[q][...] = out.reshape(shape + (chunk[q],))
         send_core(q)
-        if q >= 1:
-            send_side(q - 1)
     gather_side(grads, 1)
-    send_side(half - 1)
+    for q in range(half):
+        send_side(q)
     gather_end(grads, 1)
 
     grad_data = grads[...].reshape(total_rows, width)

time: 45.8 us -> 45.3 us (0.989)
  Pallas kernels: 45 us -> 44.5 us
    pallas_call x1, Pallas kernels: 43.4 us -> 42.9 us  [local_fused(): pl.pallas_call(functools.partial(fused_kernel, depth, chunk), out_shape=(...]
where the time goes in v4:
time: 45.3 us; the launch traced here: 45.1 us
  Pallas kernels  44.5 us (98%)
  between operations  0.64 us (1%)
    pallas_call x1, Pallas kernels, local_fused(): pl.pallas_call(functools.partial(fused_kernel, depth, chunk), out_shape=(...  42.9 us
    pallas_call x1, Pallas kernels, local_fused(): pl.pallas_call(store_kernel, out_shape=tuple((jax.ShapeDtypeStruct(r.shap...  1.53 us

profile of v4, /device:TPU:0, one launch (start us, length us, event | category | flops | bytes accessed | tf_op | source)
XLA Modules:
  0.0 45.1 jit_solution(7898727264622502058)
XLA Ops:
  0.6 42.9 %shard_map.103 = (bf16[16,2048]{1,0:T(8,128)(2,1)}, bf16[16,2048]{1,0:T(8,128)(2,1)}, f32[8,16]{1,0:T(8,128)}) custom-call(bf16[16,2048]{1,0:T(8,128)(2,1)} %tokens.1, s32[8,16]{1,0:T(8,128)} %bitcast.4, s32[8,16]{1,0:T(8,128)} %bitcast.5, f32[8,16]{1,0:T(8,128)} %bitcast.6, bf16[16,2048]{1,0:T(8,128)(2,1)} %cotangent.1, bf16[1,2048,768]{2,1,0:T(8,128)(2,1)} %gate_hbm.1, ...), custom_call_target="tpu_custom_call" | custom-call | flops 4831838208 | bytes 9437184 | tf_op jit(solution)/shard_map/pallas_call | solution.py:370
  43.6 1.5 %shard_map.104 = (bf16[16,2048]{1,0:T(8,128)(2,1)}, bf16[16,2048]{1,0:T(8,128)(2,1)}, f32[8,16]{1,0:T(8,128)}) custom-call(bf16[16,2048]{1,0:T(8,128)(2,1)} %get-tuple-element.9.refs_0_, bf16[16,2048]{1,0:T(8,128)(2,1)} %get-tuple-element.10.refs_1_, f32[8,16]{1,0:T(8,128)} %get-tuple-element.11.refs_2_), custom_call_target="tpu_custom_call" | custom-call | tf_op jit(solution)/shard_map/pallas_call | solution.py:390
